TPU v7x, 32 devices: a whole 2x2x4 slice. The times are simulated.
32 devices in a mesh: ctx: 4 (over y, x), grp: 8 (over z, core).
Axes of the slice: x: 2, y: 2, z: 4, core: 2. Of those that a mesh axis runs over, the one named last changes fastest.
Arguments:
- tokens: bfloat16 [1024, 6144], P('ctx', 'grp'), may hold values from -6 to 6
- frames: int32 [1024], replicated, may hold values from 0 to 7, never falling along the last dimension, each value on 1 to 512 neighbouring positions
- qkv_weight: bfloat16 [6144, 3072], P(None, 'grp'), may hold values from -0.15309311 to 0.15309311
- out_weight: bfloat16 [1024, 6144], P(None, 'grp'), may hold values from -0.1875 to 0.1875
- cond_weight: bfloat16 [6144, 1536], P('grp'), may hold values from -0.078125 to 0.078125
- cond_bias: float32 [1536], replicated, may hold values from -3 to 3
- in_weight: bfloat16 [16, 1536], replicated, may hold values from -1.5 to 1.5
- mid_weight: bfloat16 [1536, 1536], replicated, may hold values from -0.15625 to 0.15625
- noise_out_weight: bfloat16 [1536, 16], replicated, may hold values from -0.15625 to 0.15625
- head_gain: float32 [1536], replicated, may hold values from 0.5 to 1.5
- targets: float32 [1024, 16], P('ctx'), may hold values from -6 to 6
- noise_draws: float32 [1024, 64], P('ctx'), may hold values from -6 to 6
- timesteps: int32 [1024, 4], P('ctx'), may hold values from 0 to 999
- masked: int32 [1024], P('ctx'), may hold values 0 or 1
- routes: int32 [1024, 1], P('ctx'), may hold values from 0 to 7; in each aligned block of 256 rows (0 to 255, 256 to 511, ...) at most 48 rows name the same one
Outputs:
- hidden_state: bfloat16 [1024, 6144], P('ctx', 'grp')
- predicted_noise: float32 [1536, 64], P(('ctx', 'grp'))
Inputs may be any that keep to these rules, and one draw needn't show every extreme that they name: `frames`: frame indices never fall along the clip; each frame has 1 to 512 tokens. `routes`: within the 256 tokens of one index of ctx, at most 48 tokens name any one value, a bound that some block reaches.
All inputs are finite; a program needn't handle non-finite values. No bound on the sum of `masked` on one device may be relied on, other than what follows from the above.
Results may differ from a plain program's by a relative error of at most 0.01.
The roundings to bfloat16 on the way count: a program that leaves them out, or rounds other values in their place, can miss the bound.
Values may be sent and summed in bfloat16 or wider, within the bound.
A program may use at most 64 MiB of HBM per device.

v0:
```python
import math

import jax
import jax.numpy as jnp
from jax import lax
from jax.sharding import PartitionSpec as P


def alpha_bar(steps_float):
    return jnp.cos((steps_float / 1000.0 + 0.008) / 1.008 * (math.pi / 2)) ** 2


def time_embed(steps_float, width):
    half_width = width // 2
    freqs = jnp.exp(-math.log(10000.0) * jnp.arange(half_width, dtype=jnp.float32) / half_width)
    angles = steps_float[..., None] * freqs
    return jnp.concatenate([jnp.cos(angles), jnp.sin(angles)], axis=-1)


def head_rows(
    conditioning,
    target_rows,
    noise_rows,
    steps_float,
    in_weight,
    mid_weight,
    noise_out_weight,
    head_gain,
):
    count = conditioning.shape[0]
    latent = target_rows.shape[1]
    draws_count = steps_float.shape[1]
    width = in_weight.shape[1]
    abar = alpha_bar(steps_float)[..., None]
    noisy = jnp.sqrt(abar) * target_rows[:, None, :] + jnp.sqrt(1.0 - abar) * noise_rows.reshape(
        count, draws_count, latent
    )
    noisy = noisy.astype(jnp.bfloat16).reshape(count * draws_count, latent)
    lifted = jnp.dot(noisy, in_weight, preferred_element_type=jnp.float32).reshape(
        count, draws_count, width
    )
    lifted = lifted + conditioning[:, None, :] + time_embed(steps_float, width)
    scale = lax.rsqrt(jnp.mean(lifted * lifted, axis=-1, keepdims=True) + 1e-06)
    normed = (lifted * scale * head_gain).astype(jnp.bfloat16).reshape(count * draws_count, width)
    middle = jnp.dot(normed, mid_weight, preferred_element_type=jnp.float32)
    block = (lifted.reshape(count * draws_count, width) + jax.nn.silu(middle)).astype(jnp.bfloat16)
    result = jnp.dot(block, noise_out_weight, preferred_element_type=jnp.float32)
    return result.reshape(count, draws_count * latent)


def shards(
    tokens,
    frames,
    qkv_weight,
    out_weight,
    cond_weight,
    cond_bias,
    in_weight,
    mid_weight,
    noise_out_weight,
    head_gain,
    targets,
    noise_draws,
    timesteps,
    masked,
    routes,
):
    tok_rows = tokens.shape[0]
    head_size = qkv_weight.shape[1] // 3
    weight_rows = qkv_weight
    qkv = jnp.dot(
        lax.all_gather(tokens, "grp", axis=1, tiled=True),
        weight_rows,
        preferred_element_type=jnp.float32,
    ).astype(jnp.bfloat16)
    queries = qkv[:, :head_size]
    keys_here = qkv[:, head_size : 2 * head_size]
    values_here = qkv[:, 2 * head_size :]
    query_frames = lax.dynamic_slice_in_dim(frames, lax.axis_index("ctx") * tok_rows, tok_rows)
    score_scale = head_size ** (-0.5)
    key_part = lax.all_gather(keys_here, "ctx", axis=0, tiled=True)
    value_part = lax.all_gather(values_here, "ctx", axis=0, tiled=True)
    row_max = jnp.full((tok_rows,), -1e30, jnp.float32)
    allowed = frames[None, :] <= query_frames[:, None]
    scores = jnp.dot(queries, key_part.T, preferred_element_type=jnp.float32) * score_scale
    scores = jnp.where(allowed, scores, -1e30)
    new_max = jnp.maximum(row_max, jnp.max(scores, axis=1))
    weights_blk = jnp.where(allowed, jnp.exp(scores - new_max[:, None]), 0.0)
    row_total = jnp.sum(weights_blk, axis=1)
    weighted = jnp.dot(
        weights_blk.astype(jnp.bfloat16), value_part, preferred_element_type=jnp.float32
    )
    row_max, row_total, weighted = (new_max, row_total, weighted)
    attended = (weighted / row_total[:, None]).astype(jnp.bfloat16)
    weight_rows = out_weight
    projected = jnp.dot(
        lax.all_gather(attended, "grp", axis=1, tiled=True),
        weight_rows,
        preferred_element_type=jnp.float32,
    )
    hidden_state = (tokens.astype(jnp.float32) + projected).astype(jnp.bfloat16)
    groups = lax.axis_size("grp")
    capacity = max(2, 3 * tok_rows // (2 * groups))
    target_dev = routes[:, 0]
    onehot = (target_dev[:, None] == jnp.arange(groups, dtype=jnp.int32)[None, :]).astype(
        jnp.int32
    ) * masked[:, None]
    before = jnp.cumsum(onehot, axis=0) - onehot
    slot_rank = jnp.sum(before * onehot, axis=1)
    slot_index = jnp.where(masked == 1, target_dev * capacity + slot_rank, groups * capacity)
    chooser = slot_index[:, None] == jnp.arange(groups * capacity, dtype=jnp.int32)[None, :]
    picked = jnp.dot(
        chooser.astype(jnp.bfloat16).T, hidden_state, preferred_element_type=jnp.float32
    ).astype(jnp.bfloat16)
    conditioning = lax.psum_scatter(
        jnp.dot(picked, cond_weight, preferred_element_type=jnp.float32),
        "grp",
        scatter_dimension=0,
        tiled=True,
    )
    conditioning = conditioning + cond_bias
    own_slots = lax.dynamic_slice_in_dim(
        chooser, lax.axis_index("grp") * capacity, capacity, 1
    ).astype(jnp.float32)
    occupied = jnp.sum(own_slots, axis=0)
    target_rows = jnp.dot(own_slots.T, targets, precision=lax.Precision.HIGHEST)
    noise_rows = jnp.dot(own_slots.T, noise_draws, precision=lax.Precision.HIGHEST)
    steps_float = jnp.dot(
        own_slots.T, timesteps.astype(jnp.float32), precision=lax.Precision.HIGHEST
    )
    predictions = head_rows(
        conditioning,
        target_rows,
        noise_rows,
        steps_float,
        in_weight,
        mid_weight,
        noise_out_weight,
        head_gain,
    )
    return (hidden_state, predictions * occupied[:, None])


def solution(mesh):
    return jax.shard_map(
        shards,
        mesh=mesh,
        in_specs=(
            P("ctx", "grp"),
            P(),
            P(None, "grp"),
            P(None, "grp"),
            P("grp", None),
            P(),
            P(),
            P(),
            P(),
            P(),
            P("ctx", None),
            P("ctx", None),
            P("ctx", None),
            P("ctx"),
            P("ctx", None),
        ),
        out_specs=(P("ctx", "grp"), P(("ctx", "grp"), None)),
        check_vma=False,
    )
```

profile of v0, /device:TPU:0, one launch (start us, length us, event | category | flops | bytes accessed | tf_op | source)
XLA Modules:
  0.0 146.4 jit_solution(3396781467575577192)
XLA Ops:
  7.2 0.0 copy-start
  7.2 0.0 all-gather.2.cloned.1.call-start
  7.2 0.7 all-gather.2.cloned.1.call-update
  7.9 0.0 reduce-scatter.2.cloned.1.call-start
  8.0 0.7 fusion.25
  8.7 0.6 reduce-window.6
  9.2 0.2 slice_reduce_fusion
  9.5 0.8 dynamic_slice.6
  10.3 0.8 fusion.24
  11.0 0.7 compare_select_fusion.1
  11.7 0.0 copy-start.6
  11.7 38.9 %all-gather.2.cloned.1.call-done = bf16[256,6144]{1,0:T(8,128)(2,1)} async-done(((bf16[256,768]{1,0:T(8,128)(2,1)}), bf16[256,6144]{1,0:T(8,128)(2,1)}) %all-gather.2.cloned.1.call-update) | async-done | bytes 3145744 | tf_op jit(solution)/shard_map/all_gather | solution.py:72
  50.6 5.1 %convolution_convert_fusion.1 = bf16[256,384]{1,0:T(8,128)(2,1)S(1)} fusion(bf16[256,6144]{1,0:T(8,128)(2,1)} %all-gather.2.cloned.1.call-done, bf16[6144,384]{1,0:T(8,128)(2,1)} %param.17), kind=kOutput, calls=%fused_computation.12 | convolution fusion | flops 1208057856 | bytes 8060928 | tf_op jit(solution)/shard_map/dot_general | solution.py:71
  55.8 9.0 %all_gather.13 = bf16[1024,128]{1,0:T(8,128)(2,1)S(1)} all-gather(bf16[256,128]{1,0:T(8,128)(2,1)S(1)} %get-tuple-element.2), channel_id=1, replica_groups=mesh['ctx'=4,'grp'=8] {'ctx'}, dimensions={0}, use_global_device_ids=true | all-gather | bytes 327680 | tf_op jit(solution)/shard_map/all_gather | solution.py:81
  64.7 0.0 copy-done.6
  64.7 0.4 fusion.34
  65.1 8.9 %all_gather.14 = bf16[1024,128]{1,0:T(8,128)(2,1)S(1)} all-gather(bf16[256,128]{1,0:T(8,128)(2,1)S(1)} %get-tuple-element.3), channel_id=1, replica_groups=mesh['ctx'=4,'grp'=8] {'ctx'}, dimensions={0}, use_global_device_ids=true | all-gather | bytes 327680 | tf_op jit(solution)/shard_map/all_gather | solution.py:82
  74.1 0.4 fusion.5
  74.4 0.0 copy-start.1
  74.4 0.0 copy-start.9
  74.5 0.4 fusion.4
  74.8 14.1 %all_gather.15 = bf16[256,1024]{1,0:T(8,128)(2,1)S(1)} all-gather(bf16[256,128]{1,0:T(8,128)(2,1)S(1)} %fusion.4), channel_id=1, replica_groups=mesh['ctx'=4,'grp'=8] {'grp'}, dimensions={1}, use_global_device_ids=true | all-gather | bytes 589824 | tf_op jit(solution)/shard_map/all_gather | solution.py:97
  89.0 0.0 copy-done.1
  89.0 0.0 copy-done.9
  89.0 0.6 fusion.2
  89.6 0.0 copy-done
  89.6 0.0 copy-start.10
  89.6 2.7 %fusion.3 = f32[384,1536]{1,0:T(8,128)} fusion(bf16[768,1536]{1,0:T(8,128)(2,1)S(1)} %copy-done, bf16[256,768]{1,0:T(8,128)(2,1)S(1)} %fusion.2, s32[256]{0:T(256)S(1)} %compare_select_fusion.1), kind=kOutput, calls=%fused_computation.8 | convolution fusion | flops 1057357824 | bytes 5112832 | tf_op jit(solution)/shard_map/dot_general | solution.py:116
  92.2 0.0 copy-done.10
  92.2 0.0 copy-start.7
  92.2 0.0 copy-start.3
  92.3 0.0 copy-start.2
  92.3 0.0 reduce-scatter.2.cloned.1.call-update
  92.3 0.0 copy-start.4
  92.3 0.1 iota_compare_fusion
  92.4 0.7 convert_reduce_fusion
  93.1 0.0 copy-done.7
  93.1 0.8 fusion.27
  93.9 0.0 copy-done.3
  93.9 0.1 fusion.20
  94.0 0.0 copy-done.2
  94.0 0.8 fusion.18
  94.8 2.1 %multiply_cosine_fusion = (f32[48,4,768]{2,0,1:T(8,128)S(1)}, f32[48,4,768]{2,0,1:T(8,128)S(1)}) fusion(f32[768]{0:T(1024)S(1)} %multiply_exponential_fusion, f32[48,4]{0,1:T(4,128)S(1)} %get-tuple-element.10), kind=kLoop, calls=%fused_computation.16 | loop fusion | flops 147456 | bytes 1183488 | tf_op jit(solution)/shard_map/cos | solution.py:17
  96.9 29.4 %reduce-scatter.2.cloned.1.call-done = f32[48,1536]{1,0:T(8,128)} async-done(((f32[384,1536]{1,0:T(8,128)}), f32[48,1536]{1,0:T(8,128)}) %reduce-scatter.2.cloned.1.call-update) | async-done | bytes 294928 | tf_op jit(solution)/shard_map/reduce_scatter | solution.py:115
  126.4 0.0 copy-done.4
  126.4 1.0 broadcast_add_fusion
  127.3 1.3 multiply_reduce_fusion
  128.6 0.0 copy-start.5
  128.6 0.8 copy.23
  129.4 0.0 copy-done.5
  129.4 0.2 multiply_convert_fusion
  129.6 1.3 copy.24
  130.9 2.2 %reshape.93 = bf16[192,1536]{1,0:T(8,128)(2,1)} reshape(bf16[48,4,1536]{2,1,0:T(4,128)(2,1)} %copy.24) | data formatting | bytes 1179648 | tf_op jit(solution)/shard_map/reshape | solution.py:44
  133.1 1.4 reshape.92
  134.5 0.0 copy-start.8
  134.5 4.3 %fusion.7 = f32[192,16]{1,0:T(8,128)S(1)} fusion(bf16[1536,16]{0,1:T(8,128)(2,1)} %param.23, f32[192,1536]{1,0:T(8,128)} %reshape.92, bf16[192,1536]{1,0:T(8,128)(2,1)} %reshape.93, bf16[1536,1536]{1,0:T(8,128)(2,1)} %param.22), kind=kOutput, calls=%fused_computation.19 | convolution fusion | flops 917176320 | bytes 6549504 | tf_op jit(solution)/shard_map/dot_general | solution.py:47
  138.8 0.1 reshape.94
  138.9 0.0 copy-done.8
  138.9 0.7 broadcast_multiply_fusion
  (6 shorter events, 0.1 us)
Async XLA Ops:
  7.2 82.4 %copy-start = (bf16[768,1536]{1,0:T(8,128)(2,1)S(1)}, bf16[768,1536]{1,0:T(8,128)(2,1)}, u32[]{:S(2)}) copy-start(bf16[768,1536]{1,0:T(8,128)(2,1)} %param.19) | copy-start | bytes 7077892
  7.2 43.5 %all-gather.2.cloned.1.call-start = ((), (), s32[]{:S(2)}) async-start(), calls=%async_computation.1 | async-start | bytes 3538944 | tf_op jit(solution)/shard_map/all_gather | solution.py:72
  7.9 118.4 %reduce-scatter.2.cloned.1.call-start = ((), (), s32[]{:S(2)}) async-start(), calls=%async_computation.2 | async-start | bytes 2654208 | tf_op jit(solution)/shard_map/reduce_scatter | solution.py:115
  11.7 53.0 %copy-start.6 = (s32[1024]{0:T(1024)S(1)}, s32[1024]{0:T(1024)}, u32[]{:S(2)}) copy-start(s32[1024]{0:T(1024)} %param.16) | copy-start | bytes 12292
  74.4 14.6 %copy-start.1 = (bf16[256,768]{1,0:T(8,128)(2,1)S(1)}, bf16[256,768]{1,0:T(8,128)(2,1)}, u32[]{:S(2)}) copy-start(bf16[256,768]{1,0:T(8,128)(2,1)} %param.15) | copy-start | bytes 1179652
  74.4 14.5 %copy-start.9 = (bf16[1024,768]{1,0:T(8,128)(2,1)S(1)}, bf16[1024,768]{1,0:T(8,128)(2,1)}, u32[]{:S(2)}) copy-start(bf16[1024,768]{1,0:T(8,128)(2,1)} %param.18) | copy-start | bytes 4718596
  89.6 2.7 %copy-start.10 = (bf16[256,768]{1,0:T(8,128)(2,1)}, bf16[256,768]{1,0:T(8,128)(2,1)S(1)}, u32[]{:S(2)}) copy-start(bf16[256,768]{1,0:T(8,128)(2,1)S(1)} %fusion.2) | copy-start | bytes 1179652
  92.2 0.8 copy-start.7
  92.2 1.6 %copy-start.3 = (f32[256,16]{0,1:T(8,128)S(1)}, f32[256,16]{0,1:T(8,128)}, u32[]{:S(2)}) copy-start(f32[256,16]{0,1:T(8,128)} %param.25) | copy-start | bytes 49156
  92.3 1.8 %copy-start.2 = (f32[256,64]{0,1:T(8,128)S(1)}, f32[256,64]{0,1:T(8,128)}, u32[]{:S(2)}) copy-start(f32[256,64]{0,1:T(8,128)} %param.26) | copy-start | bytes 196612
  92.3 34.1 %copy-start.4 = (f32[1536]{0:T(1024)S(1)}, f32[1536]{0:T(1024)}, u32[]{:S(2)}) copy-start(f32[1536]{0:T(1024)} %param.20) | copy-start | bytes 18436
  128.6 0.8 copy-start.5
  134.5 4.4 %copy-start.8 = (f32[48]{0:T(128)S(1)}, f32[48]{0:T(128)}, u32[]{:S(2)}) copy-start(f32[48]{0:T(128)} %convert_reduce_fusion) | copy-start | bytes 580
Sparse Core Ops, SparseCore 0:
  9.6 40.9 all-gather.1
  92.4 33.9 reduce-scatter.1
where the time goes:
time: 147 us; the launch traced here: 146 us
  waiting for transfers between devices  69 us (47%)
  blocking collectives  32 us (22%)
  matrix products  16.3 us (11%)
  between operations  14.2 us (10%)
  other arithmetic  7.89 us (5%)
  local copies, waits for them, and re-layouts  6.81 us (5%)
    all_gather x1, waiting for transfers between devices, shards(): lax.all_gather(tokens, 'grp', axis=1, tiled=True)  38.9 us
    reduce_scatter x1, waiting for transfers between devices, shards(): lax.psum_scatter(jnp.dot(picked, cond_weight, preferred_element_type=jnp....  29.4 us
    all_gather x1, blocking collectives, shards(): lax.all_gather(attended, 'grp', axis=1, tiled=True)  14.1 us
    all_gather x1, blocking collectives, shards(): key_part = lax.all_gather(keys_here, 'ctx', axis=0, tiled=True)  8.95 us
    all_gather x1, blocking collectives, shards(): value_part = lax.all_gather(values_here, 'ctx', axis=0, tiled=True)  8.95 us
    dot_general x1, matrix products, shards(): jnp.dot(lax.all_gather(tokens, 'grp', axis=1, tiled=True), weight_rows, p...  5.09 us
    dot_general x1, matrix products, head_rows(): jnp.dot(block, noise_out_weight, preferred_element_type=jnp.float32)  4.25 us
  transfers between devices with their start and end apart: 2, of which 2 were waited for; matrix products, arithmetic and copies ran while one was open for 6% of the time, Pallas kernels for 0%

commit v1 on v0

v1 whole, which is shorter than its diff:
```python
import functools
import math

import jax
import jax.numpy as jnp
import numpy as np
from jax import lax
from jax.experimental import pallas as pl
from jax.experimental.pallas import tpu as pltpu
from jax.sharding import PartitionSpec as P

MESH = pl.DeviceIdType.MESH
F32 = jnp.float32
BF16 = jnp.bfloat16
ROW_PARTS = 2


def dot(a, b):
    return jnp.dot(a, b, preferred_element_type=F32)


def kernel(
    n_ctx,
    n_grp,
    cap,
    rows_cap,
    tokens,
    frames,
    qkv_w,
    out_w,
    cond_w,
    bias,
    in_w,
    mid_w,
    noise_out,
    gain,
    targets,
    noise,
    steps,
    masked,
    routes,
    freqs,
    hid_out,
    pred_out,
    tok_all,
    qkv_wv,
    out_wv,
    cond_wv,
    mid_wv,
    kv_all,
    q_own,
    att_all,
    hid,
    acc,
    base,
    normed,
    slot_row,
    mine,
    sib_send,
    sib_recv,
    rs_send,
    rs_recv,
    load_sem,
    up_s,
    up_r,
    fw_s,
    fw_r,
    kv_s,
    kv_r,
    at_s,
    at_r,
    af_s,
    af_r,
    sb_s,
    sb_r,
    rs_s,
    rs_r,
):
    ctx = lax.axis_index("ctx")
    grp = lax.axis_index("grp")
    pairs = n_grp // 2
    pair, core = grp // 2, grp % 2
    sibling = grp + 1 - 2 * core
    tok_rows, d_shard = tokens.shape
    head = q_own.shape[1]
    width = in_w.shape[1]
    latent = targets.shape[1]
    draws = steps.shape[1]
    part = tok_rows // ROW_PARTS
    col = width // rs_s.shape[0]
    n_cols = rs_s.shape[0]

    def remote(src, dst, send, recv, to):
        return pltpu.make_async_remote_copy(
            src_ref=src, dst_ref=dst, send_sem=send, recv_sem=recv, device_id=to, device_id_type=MESH
        )

    def same_core(offset):
        return ((pair + offset + pairs) % pairs) * 2 + core

    loads = [
        pltpu.make_async_copy(src, dst, load_sem.at[i])
        for i, (src, dst) in enumerate(
            (
                (tokens, tok_all.at[grp]),
                (qkv_w, qkv_wv),
                (out_w, out_wv),
                (cond_w, cond_wv),
                (mid_w, mid_wv),
            )
        )
    ]
    loads[0].start()

    barrier = pltpu.get_barrier_semaphore()
    peers = [(ctx, same_core(j)) for j in range(1, pairs)]
    peers += [(ctx, sibling)]
    peers += [((ctx + j) % n_ctx, grp) for j in range(1, n_ctx)]
    for peer in peers:
        pl.semaphore_signal(barrier, inc=1, device_id=peer, device_id_type=MESH)
    for load in loads[1:]:
        load.start()
    pl.semaphore_wait(barrier, len(peers))
    loads[0].wait()

    def piece(shard, k):
        return tok_all.at[shard, pl.ds(k * part, part)]

    def chain(way, step, k):
        sign = 1 if way == 0 else -1
        shard = jnp.clip(pair - sign * step, 0, pairs - 1) * 2 + core
        to = jnp.clip(pair + sign, 0, pairs - 1) * 2 + core
        ref = piece(shard, k)
        return remote(ref, ref, up_s.at[way, step, k], up_r.at[way, step, k], (ctx, to))

    def chain_in(way, step, k):
        sign = 1 if way == 0 else -1
        shard = jnp.clip(pair - sign * (step + 1), 0, pairs - 1) * 2 + core
        ref = piece(shard, k)
        return remote(ref, ref, up_s.at[way, step, k], up_r.at[way, step, k], (ctx, sibling))

    def sends(way, step):
        if way == 0:
            return (pair - step >= 0) & (pair + 1 < pairs)
        return (pair + step < pairs) & (pair >= 1)

    def gets(way, step):
        if way == 0:
            return pair - 1 - step >= 0
        return pair + 1 + step < pairs

    def forward(way, step, k, from_sibling=False):
        sign = 1 if way == 0 else -1
        shard = jnp.clip(pair - sign * step, 0, pairs - 1) * 2 + (1 - core if from_sibling else core)
        ref = piece(shard, k)
        return remote(ref, ref, fw_s.at[way, step, k], fw_r.at[way, step, k], (ctx, sibling))

    for k in range(ROW_PARTS):
        for way in (0, 1):

            @pl.when(sends(way, 0))
            def _():
                chain(way, 0, k).start()

    for k in range(ROW_PARTS):
        forward(0, 0, k).start()

    def add_qkv(shard, k, first=False):
        weight = qkv_wv[pl.ds(pl.multiple_of(shard * d_shard, d_shard), d_shard), :]
        rows = pl.ds(k * part, part)
        term = dot(tok_all[shard, k * part : (k + 1) * part, :], weight)
        acc[rows, :] = term if first else acc[rows, :] + term

    def slots_of():
        mask = masked[...]
        route = routes[...]
        shape = (n_grp, tok_rows)
        onehot = jnp.where((lax.broadcasted_iota(jnp.int32, shape, 0) == route) & (mask == 1), 1.0, 0.0)
        square = (tok_rows, tok_rows)
        earlier = lax.broadcasted_iota(jnp.int32, square, 0) < lax.broadcasted_iota(jnp.int32, square, 1)
        before = dot(onehot.astype(BF16), jnp.where(earlier, 1.0, 0.0).astype(BF16))
        rank = jnp.sum(before * onehot, axis=0, keepdims=True).astype(jnp.int32)
        slot_row[...] = jnp.where(mask == 1, route * rows_cap + rank, -1)

    def own_slots():
        want = lax.broadcasted_iota(jnp.int32, (rows_cap, tok_rows), 0) + grp * rows_cap
        return jnp.where(want == slot_row[...], 1.0, 0.0)

    def draw_base(k):
        own = own_slots().astype(BF16)
        step = steps[:, k : k + 1]
        stepf = step.astype(F32)
        abar = jnp.cos((stepf / 1000.0 + 0.008) / 1.008 * (math.pi / 2)) ** 2
        lanes = slice(k * latent, (k + 1) * latent)
        noisy = (jnp.sqrt(abar) * targets[...] + jnp.sqrt(1.0 - abar) * noise[:, lanes]).astype(BF16)
        picked = dot(own, noisy).astype(BF16)
        high = (step >> 5).astype(F32)
        low = (step & 31).astype(F32)
        s = dot(own, high.astype(BF16)) * 32.0 + dot(own, low.astype(BF16))
        rows = slice(k * rows_cap, (k + 1) * rows_cap)
        angles = s * freqs[...]
        half = width // 2
        base[rows, :half] = dot(picked, in_w[:, :half]) + jnp.cos(angles) + bias[:, :half]
        base[rows, half:] = dot(picked, in_w[:, half:]) + jnp.sin(angles) + bias[:, half:]

    work = [functools.partial(draw_base, k) for k in range(draws)]
    slots_of()
    loads[1].wait()
    for k in range(ROW_PARTS):
        add_qkv(grp, k, first=True)

    for step in range(pairs - 1):
        for k in range(ROW_PARTS):
            for way in (0, 1):

                @pl.when(gets(way, step))
                def _():
                    chain_in(way, step, k).wait_recv()

                if step + 1 < pairs - 1:

                    @pl.when(sends(way, step + 1))
                    def _():
                        chain(way, step + 1, k).start()

                @pl.when(gets(way, step))
                def _():
                    forward(way, step + 1, k).start()
                    sign = 1 if way == 0 else -1
                    add_qkv((pair - sign * (step + 1)) * 2 + core, k)

            for way in (0, 1) if step else (0,):

                @pl.when(True if step == 0 else gets(way, step - 1))
                def _():
                    forward(way, step, k, True).wait_recv()
                    sign = 1 if way == 0 else -1
                    add_qkv((pair - sign * step) * 2 + 1 - core, k)

            if work:
                work.pop(0)()
    while work:
        work.pop(0)()
    for k in range(ROW_PARTS):
        for way in (0, 1):

            @pl.when(gets(way, pairs - 2))
            def _():
                forward(way, pairs - 1, k, True).wait_recv()
                sign = 1 if way == 0 else -1
                add_qkv((pair - sign * (pairs - 1)) * 2 + 1 - core, k)

    kv_all[0] = acc[:, head:].astype(BF16)
    kv_copies = []
    for j in range(1, n_ctx):
        copy = remote(kv_all.at[0], kv_all.at[j], kv_s.at[j], kv_r.at[j], ((ctx + j) % n_ctx, grp))
        copy.start()
        kv_copies.append(copy)
    q = acc[:, :head].astype(BF16)
    mine_frames = frames[:, pl.ds(pl.multiple_of(ctx * tok_rows, tok_rows), tok_rows)]
    square = (tok_rows, tok_rows)
    same = lax.broadcasted_iota(jnp.int32, square, 0) == lax.broadcasted_iota(jnp.int32, square, 1)
    frame_col = jnp.sum(jnp.where(same, mine_frames, 0), axis=1, keepdims=True)
    scores = []
    for j in range(n_ctx):
        if j:
            kv_copies[j - 1].wait_recv()
        block = (ctx + n_ctx - j) % n_ctx
        frame_row = frames[:, pl.ds(pl.multiple_of(block * tok_rows, tok_rows), tok_rows)]
        s = lax.dot_general(
            q, kv_all[j, :, :head], (((1,), (1,)), ((), ())), preferred_element_type=F32
        ) * (head**-0.5)
        scores.append(jnp.where(frame_row <= frame_col, s, -1e30))
    top = functools.reduce(jnp.maximum, [jnp.max(s, axis=1, keepdims=True) for s in scores])
    total = jnp.zeros((tok_rows, 1), F32)
    weighted = jnp.zeros((tok_rows, head), F32)
    for j in range(n_ctx):
        w = jnp.exp(scores[j] - top)
        total = total + jnp.sum(w, axis=1, keepdims=True)
        weighted = weighted + dot(w.astype(BF16), kv_all[j, :, head:])

    def heads(index):
        return att_all.at[:, pl.ds(pl.multiple_of(index * head, head), head)]

    q_own[...] = (weighted / total).astype(BF16)
    att_all[:, pl.ds(pl.multiple_of(grp * head, head), head)] = q_own[...]
    att_copies = []
    for j in range(1, pairs):
        copy = remote(q_own, heads(grp), at_s.at[j], at_r.at[j], (ctx, same_core(j)))
        copy.start()
        att_copies.append(copy)
    att_fw = [remote(q_own, heads(grp), af_s.at[0], af_r.at[0], (ctx, sibling))]
    att_fw[0].start()
    for j in range(1, pairs):
        got = heads(same_core(-j))
        remote(got, got, at_s.at[j], at_r.at[j], (ctx, sibling)).wait_recv()
        copy = remote(got, got, af_s.at[j], af_r.at[j], (ctx, sibling))
        copy.start()
        att_fw.append(copy)
    loads[2].wait()
    for j in range(pairs):
        got = heads(same_core(-j) + 1 - 2 * core)
        remote(got, got, af_s.at[j], af_r.at[j], (ctx, sibling)).wait_recv()
    projected = dot(att_all[...], out_wv[...])
    hidden = (tok_all[grp].astype(F32) + projected).astype(BF16)
    hid_out[...] = hidden
    hid[...] = hidden

    loads[3].wait()
    row = slot_row[...]
    slots_shape = (pairs * rows_cap, tok_rows)
    place = lax.broadcasted_iota(jnp.int32, slots_shape, 0)
    route = routes[...]
    pair_slot = row - route * rows_cap + (route >> 1) * rows_cap
    mine_row = jnp.where((row >= 0) & ((route & 1) == core), pair_slot, -1)
    sib_row = jnp.where((row >= 0) & ((route & 1) != core), pair_slot, -1)
    choose_mine = jnp.where(place == mine_row, 1.0, 0.0).astype(BF16)
    choose_sib = jnp.where(place == sib_row, 1.0, 0.0).astype(BF16)
    sib_copies = []
    for k in range(n_cols):
        cols = slice(k * col, (k + 1) * col)
        by_token = dot(hid[...], cond_wv[:, cols]).astype(BF16)
        sib_send[k] = dot(choose_sib, by_token).astype(BF16)
        copy = remote(sib_send.at[k], sib_recv.at[k], sb_s.at[k], sb_r.at[k], (ctx, sibling))
        copy.start()
        sib_copies.append(copy)
        mine[k] = dot(choose_mine, by_token)
    rs_copies = []
    for k in range(n_cols):
        sib_copies[k].wait_recv()
        summed = mine[k] + sib_recv[k].astype(F32)
        mine[k] = summed
        rs_send[k] = summed.astype(BF16)
        for j in range(1, pairs):
            to = (pair + j) % pairs
            rows = pl.ds(pl.multiple_of(to * rows_cap, rows_cap), rows_cap)
            copy = remote(
                rs_send.at[k, rows], rs_recv.at[k, j], rs_s.at[k, j], rs_r.at[k, j], (ctx, to * 2 + core)
            )
            copy.start()
            rs_copies.append(copy)

    squares = [jnp.zeros((rows_cap, 1), F32) for _ in range(draws)]
    for k in range(n_cols):
        cols = slice(k * col, (k + 1) * col)
        cond = mine[k, pl.ds(pl.multiple_of(pair * rows_cap, rows_cap), rows_cap), :]
        for j in range(1, pairs):
            rs_copies[k * (pairs - 1) + j - 1].wait_recv()
            cond = cond + rs_recv[k, j].astype(F32)
        for d in range(draws):
            rows = slice(d * rows_cap, (d + 1) * rows_cap)
            lifted = base[rows, cols] + cond
            base[rows, cols] = lifted
            squares[d] = squares[d] + jnp.sum(lifted * lifted, axis=1, keepdims=True)
    for d in range(draws):
        rows = slice(d * rows_cap, (d + 1) * rows_cap)
        scale = lax.rsqrt(squares[d] / width + 1e-06)
        normed[rows, :] = (base[rows, :] * scale * gain[...]).astype(BF16)
    loads[4].wait()

    def middle_cols(i, total):
        start = pl.multiple_of(i * 256, 256)
        middle = dot(normed[...], mid_wv[:, pl.ds(start, 256)])
        block = (base[:, pl.ds(start, 256)] + middle / (1.0 + jnp.exp(-middle))).astype(BF16)
        return total + dot(block, noise_out[pl.ds(start, 256), :])

    result = lax.fori_loop(0, width // 256, middle_cols, jnp.zeros((draws * rows_cap, latent), F32))
    occupied = jnp.sum(own_slots(), axis=1, keepdims=True)
    for d in range(draws):
        block = result[d * rows_cap : (d + 1) * rows_cap] * occupied
        pred_out[:, d * latent : (d + 1) * latent] = block[:cap]

    for k in range(ROW_PARTS):
        forward(0, 0, k).wait_send()
        for way in (0, 1):
            for step in range(pairs - 1):

                @pl.when(sends(way, step))
                def _():
                    chain(way, step, k).wait_send()

                @pl.when(gets(way, step))
                def _():
                    forward(way, step + 1, k).wait_send()

    for copy in kv_copies + att_copies + att_fw + sib_copies + rs_copies:
        copy.wait_send()


def shards(n_ctx, n_grp, *arrays):
    (tokens, frames, qkv_w, out_w, cond_w, bias, in_w, mid_w, noise_out, gain) = arrays[:10]
    targets, noise, steps, masked, routes = arrays[10:]
    tok_rows, d_shard = tokens.shape
    head = qkv_w.shape[1] // 3
    width = in_w.shape[1]
    draws = steps.shape[1]
    pairs = n_grp // 2
    cap = max(2, 3 * tok_rows // (2 * n_grp))
    rows_cap = -(-cap // 16) * 16
    n_cols = 3
    col = width // n_cols
    half = width // 2
    freqs = np.exp(-math.log(10000.0) * np.arange(half, dtype=np.float32) / half).astype(np.float32)
    vmem = pl.BlockSpec(memory_space=pltpu.VMEM)
    hbm = pl.BlockSpec(memory_space=pl.ANY)
    dma = pltpu.SemaphoreType.DMA
    chain = dma((2, pairs - 1, ROW_PARTS))
    fwd = dma((2, pairs, ROW_PARTS))
    ops = (
        tokens,
        frames.reshape(1, -1),
        qkv_w,
        out_w,
        cond_w,
        bias.reshape(1, -1),
        in_w,
        mid_w,
        noise_out,
        gain.reshape(1, -1),
        targets,
        noise,
        steps,
        masked.reshape(1, -1),
        routes.reshape(1, -1),
        jnp.asarray(freqs).reshape(1, -1),
    )
    specs = [hbm if i in (0, 2, 3, 4, 7) else vmem for i in range(len(ops))]
    return pl.pallas_call(
        functools.partial(kernel, n_ctx, n_grp, cap, rows_cap),
        out_shape=(
            jax.ShapeDtypeStruct(tokens.shape, BF16),
            jax.ShapeDtypeStruct((cap, noise.shape[1]), F32),
        ),
        in_specs=specs,
        out_specs=(vmem, vmem),
        scratch_shapes=[
            pltpu.VMEM((n_grp, tok_rows, d_shard), BF16),
            pltpu.VMEM(qkv_w.shape, BF16),
            pltpu.VMEM(out_w.shape, BF16),
            pltpu.VMEM(cond_w.shape, BF16),
            pltpu.VMEM(mid_w.shape, BF16),
            pltpu.VMEM((n_ctx, tok_rows, 2 * head), BF16),
            pltpu.VMEM((tok_rows, head), BF16),
            pltpu.VMEM((tok_rows, n_grp * head), BF16),
            pltpu.VMEM((tok_rows, d_shard), BF16),
            pltpu.VMEM((tok_rows, 3 * head), F32),
            pltpu.VMEM((draws * rows_cap, width), F32),
            pltpu.VMEM((draws * rows_cap, width), BF16),
            pltpu.VMEM((1, tok_rows), jnp.int32),
            pltpu.VMEM((n_cols, pairs * rows_cap, col), F32),
            pltpu.VMEM((n_cols, pairs * rows_cap, col), BF16),
            pltpu.VMEM((n_cols, pairs * rows_cap, col), BF16),
            pltpu.VMEM((n_cols, pairs * rows_cap, col), BF16),
            pltpu.VMEM((n_cols, pairs, rows_cap, col), BF16),
            dma((5,)),
            chain,
            chain,
            fwd,
            fwd,
            dma((n_ctx,)),
            dma((n_ctx,)),
            dma((pairs,)),
            dma((pairs,)),
            dma((pairs,)),
            dma((pairs,)),
            dma((n_cols,)),
            dma((n_cols,)),
            dma((n_cols, pairs)),
            dma((n_cols, pairs)),
        ],
        compiler_params=pltpu.CompilerParams(
            collective_id=0, has_side_effects=True, vmem_limit_bytes=52 * 2**20
        ),
    )(*ops)


def solution(mesh):
    return jax.shard_map(
        functools.partial(shards, mesh.shape["ctx"], mesh.shape["grp"]),
        mesh=mesh,
        in_specs=(
            P("ctx", "grp"),
            P(),
            P(None, "grp"),
            P(None, "grp"),
            P("grp", None),
            P(),
            P(),
            P(),
            P(),
            P(),
            P("ctx", None),
            P("ctx", None),
            P("ctx", None),
            P("ctx"),
            P("ctx", None),
        ),
        out_specs=(P("ctx", "grp"), P(("ctx", "grp"), None)),
        check_vma=False,
    )
```

time: 147 us -> 83 us (0.56)
  Pallas kernels: 0 us -> 70.9 us
  waiting for transfers between devices: 69 us -> 0 us
  blocking collectives: 32 us -> 0 us
  matrix products: 16.3 us -> 0 us
  between operations: 14.2 us -> 0.67 us
  other arithmetic: 7.89 us -> 0 us
  local copies, waits for them, and re-layouts: 6.81 us -> 10.9 us
    pallas_call x0 -> x1, Pallas kernels: none -> 70.9 us  [shards(): pl.pallas_call(functools.partial(kernel, n_ctx, n_grp, cap, rows_cap), ou...]
    all_gather x1 -> x0, waiting for transfers between devices: 38.9 us -> none  [shards(): lax.all_gather(tokens, 'grp', axis=1, tiled=True)]
    all_gather x3 -> x0, blocking collectives: 32 us -> none  [the longest x1 14.1 us: shards(): lax.all_gather(attended, 'grp', axis=1, tiled=True)]
    reduce_scatter x1 -> x0, waiting for transfers between devices: 29.4 us -> none  [shards(): lax.psum_scatter(jnp.dot(picked, cond_weight, preferred_element_type=jnp....]
    dot_general x10 -> x0, matrix products: 16.3 us -> none  [the longest x1 5.09 us: shards(): jnp.dot(lax.all_gather(tokens, 'grp', axis=1, tiled=True), weight_rows, p...]
    unnamed x22 -> x18, local copies, waits for them, and re-layouts: 0.06 us -> 9.46 us
    reshape x3 -> x2, local copies, waits for them, and re-layouts: 3.73 us -> 1.4 us  [the longest x1 0.7 us: shards(): bias.reshape(1, -1)]
    cos x1 -> x0, other arithmetic: 2.11 us -> none  [time_embed(): return jnp.concatenate([jnp.cos(angles), jnp.sin(angles)], axis=-1)]
  transfers between devices with their start and end apart: 2 -> 0, of which waited for: 2 -> 0; matrix products, arithmetic and copies ran while one was open for 6% -> 0% of each run, Pallas kernels for 0% -> 0%
where the time goes in v1:
time: 83 us; the launch traced here: 82.5 us
  Pallas kernels  70.9 us (85%)
  local copies, waits for them, and re-layouts  10.9 us (13%)
    pallas_call x1, Pallas kernels, shards(): pl.pallas_call(functools.partial(kernel, n_ctx, n_grp, cap, rows_cap), ou...  70.9 us
    unnamed x18, local copies, waits for them, and re-layouts  9.46 us

profile of v1, /device:TPU:0, one launch (start us, length us, event | category | flops | bytes accessed | tf_op | source)
XLA Modules:
  0.0 82.5 jit_solution(3714816270781338908)
XLA Ops:
  0.6 0.7 reshape.23.bias
  1.3 0.7 reshape.24.gain
  2.0 0.8 copy.19.targets
  2.8 0.9 %copy.20.noise = f32[256,64]{1,0:T(8,128)S(1)} copy(f32[256,64]{0,1:T(8,128)} %param.27) | data formatting | bytes 131072 | tf_op args[11]
  3.8 0.8 copy.21.steps
  4.6 1.0 %copy.18.noise_out = bf16[1536,16]{1,0:T(8,128)(2,1)S(1)} copy(bf16[1536,16]{0,1:T(8,128)(2,1)} %param.24) | data formatting | bytes 98304 | tf_op args[8]
  5.6 0.0 copy-start
  5.7 1.0 %copy-done = bf16[256,768]{1,0:T(8,128)(2,1)S(1)} copy-done((bf16[256,768]{1,0:T(8,128)(2,1)S(1)}, bf16[256,768]{1,0:T(8,128)(2,1)}, u32[]{:S(2)}) %copy-start) | copy-done | bytes 393240
  6.6 0.0 copy-start.1
  6.6 0.8 copy-done.1
  7.4 0.0 copy-start.2
  7.4 0.7 copy-done.2
  8.1 0.0 copy-start.3
  8.1 0.7 copy-done.3
  8.8 0.0 copy-start.4
  8.8 0.7 copy-done.4
  9.5 0.0 copy-start.5
  9.5 0.7 copy-done.5
  10.2 70.9 %shard_map.167 = (bf16[256,768]{1,0:T(8,128)(2,1)S(1)}, f32[48,64]{1,0:T(8,128)S(1)}) custom-call(bf16[256,768]{1,0:T(8,128)(2,1)S(1)} %copy-done, s32[1,1024]{1,0:T(1,128)S(1)} %bitcast.3, bf16[6144,384]{1,0:T(8,128)(2,1)} %qkv_w.1, bf16[1024,768]{1,0:T(8,128)(2,1)} %out_w.1, bf16[768,1536]{1,0:T(8,128)(2,1)} %cond_w.1, f32[1,1536]{1,0:T(1,128)S(1)} %reshape.23.bias, ...), custom_call_target="tpu_custom_call" | custom-call | tf_op jit(solution)/shard_map/pallas_call | solution.py:428
  81.1 0.7 copy.24
  81.8 0.6 copy.25
Async XLA Ops:
  5.6 1.0 %copy-start = (bf16[256,768]{1,0:T(8,128)(2,1)S(1)}, bf16[256,768]{1,0:T(8,128)(2,1)}, u32[]{:S(2)}) copy-start(bf16[256,768]{1,0:T(8,128)(2,1)} %tokens.1) | copy-start | bytes 1179652
  6.6 0.8 copy-start.1
  7.4 0.7 copy-start.2
  8.1 0.7 copy-start.3
  8.8 0.7 copy-start.4
  9.5 0.7 copy-start.5

commit v2 on v1

--- a/solution.py
+++ b/solution.py
@@ -25,23 +25,34 @@
     cap,
     rows_cap,
     tokens,
-    frames,
+    frames_h,
     qkv_w,
     out_w,
     cond_w,
-    bias,
+    bias_h,
+    in_w_h,
+    mid_w,
+    noise_out_h,
+    gain_h,
+    targets_h,
+    noise_h,
+    steps_h,
+    masked_h,
+    routes_h,
+    freqs_h,
+    hid_out,
+    pred_out,
+    frames,
+    bias_rows,
     in_w,
-    mid_w,
     noise_out,
-    gain,
+    gain_rows,
     targets,
     noise,
     steps,
     masked,
     routes,
-    freqs,
-    hid_out,
-    pred_out,
+    freqs_rows,
     tok_all,
     qkv_wv,
     out_wv,
@@ -54,6 +65,8 @@
     acc,
     base,
     normed,
+    step_slots,
+    picked,
     slot_row,
     mine,
     sib_send,
@@ -61,6 +74,7 @@
     rs_send,
     rs_recv,
     load_sem,
+    small_sem,
     up_s,
     up_r,
     fw_s,
@@ -84,8 +98,8 @@
     tok_rows, d_shard = tokens.shape
     head = q_own.shape[1]
     width = in_w.shape[1]
-    latent = targets.shape[1]
-    draws = steps.shape[1]
+    latent = targets.shape[0]
+    draws = steps.shape[0]
     part = tok_rows // ROW_PARTS
     col = width // rs_s.shape[0]
     n_cols = rs_s.shape[0]
@@ -111,6 +125,27 @@
         )
     ]
     loads[0].start()
+    smalls = [
+        pltpu.make_async_copy(src, dst, small_sem.at[i])
+        for i, (src, dst) in enumerate(
+            (
+                (masked_h, masked),
+                (routes_h, routes),
+                (targets_h, targets),
+                (noise_h, noise),
+                (steps_h, steps),
+                (freqs_h, freqs_rows),
+                (in_w_h, in_w),
+                (bias_h, bias_rows),
+                (frames_h, frames),
+                (gain_h, gain_rows),
+                (noise_out_h, noise_out),
+            )
+        )
+    ]
+
+    def row_of(ref):
+        return jnp.concatenate([ref[i : i + 1, :] for i in range(ref.shape[0])], axis=1)
 
     barrier = pltpu.get_barrier_semaphore()
     peers = [(ctx, same_core(j)) for j in range(1, pairs)]
@@ -118,7 +153,7 @@
     peers += [((ctx + j) % n_ctx, grp) for j in range(1, n_ctx)]
     for peer in peers:
         pl.semaphore_signal(barrier, inc=1, device_id=peer, device_id_type=MESH)
-    for load in loads[1:]:
+    for load in loads[1:2] + smalls + loads[2:]:
         load.start()
     pl.semaphore_wait(barrier, len(peers))
     loads[0].wait()
@@ -186,24 +221,34 @@
         want = lax.broadcasted_iota(jnp.int32, (rows_cap, tok_rows), 0) + grp * rows_cap
         return jnp.where(want == slot_row[...], 1.0, 0.0)
 
+    def noisy_of():
+        own = own_slots().astype(BF16)
+        step = steps[...]
+        pick = (((1,), (1,)), ((), ()))
+        high = (step >> 5).astype(F32).astype(BF16)
+        low = (step & 31).astype(F32).astype(BF16)
+        step_slots[...] = lax.dot_general(
+            own, high, pick, preferred_element_type=F32
+        ) * 32.0 + lax.dot_general(own, low, pick, preferred_element_type=F32)
+        abar = jnp.cos((step.astype(F32) / 1000.0 + 0.008) / 1.008 * (math.pi / 2)) ** 2
+        keep, add = jnp.sqrt(abar), jnp.sqrt(1.0 - abar)
+        for k in range(draws):
+            drawn = noise[k * latent : (k + 1) * latent, :]
+            noisy = (keep[k : k + 1] * targets[...] + add[k : k + 1] * drawn).astype(BF16)
+            rows = slice(k * rows_cap, (k + 1) * rows_cap)
+            picked[rows, :] = lax.dot_general(own, noisy, pick, preferred_element_type=F32).astype(BF16)
+
     def draw_base(k):
-        own = own_slots().astype(BF16)
-        step = steps[:, k : k + 1]
-        stepf = step.astype(F32)
-        abar = jnp.cos((stepf / 1000.0 + 0.008) / 1.008 * (math.pi / 2)) ** 2
-        lanes = slice(k * latent, (k + 1) * latent)
-        noisy = (jnp.sqrt(abar) * targets[...] + jnp.sqrt(1.0 - abar) * noise[:, lanes]).astype(BF16)
-        picked = dot(own, noisy).astype(BF16)
-        high = (step >> 5).astype(F32)
-        low = (step & 31).astype(F32)
-        s = dot(own, high.astype(BF16)) * 32.0 + dot(own, low.astype(BF16))
         rows = slice(k * rows_cap, (k + 1) * rows_cap)
-        angles = s * freqs[...]
+        angles = step_slots[:, k : k + 1] * row_of(freqs_rows)
         half = width // 2
-        base[rows, :half] = dot(picked, in_w[:, :half]) + jnp.cos(angles) + bias[:, :half]
-        base[rows, half:] = dot(picked, in_w[:, half:]) + jnp.sin(angles) + bias[:, half:]
-
-    work = [functools.partial(draw_base, k) for k in range(draws)]
+        bias = row_of(bias_rows)
+        base[rows, :half] = dot(picked[rows, :], in_w[:, :half]) + jnp.cos(angles) + bias[:, :half]
+        base[rows, half:] = dot(picked[rows, :], in_w[:, half:]) + jnp.sin(angles) + bias[:, half:]
+
+    work = [noisy_of] + [functools.partial(draw_base, k) for k in range(draws)]
+    for load in smalls:
+        load.wait()
     slots_of()
     loads[1].wait()
     for k in range(ROW_PARTS):
@@ -317,16 +362,9 @@
     choose_mine = jnp.where(place == mine_row, 1.0, 0.0).astype(BF16)
     choose_sib = jnp.where(place == sib_row, 1.0, 0.0).astype(BF16)
     sib_copies = []
-    for k in range(n_cols):
-        cols = slice(k * col, (k + 1) * col)
-        by_token = dot(hid[...], cond_wv[:, cols]).astype(BF16)
-        sib_send[k] = dot(choose_sib, by_token).astype(BF16)
-        copy = remote(sib_send.at[k], sib_recv.at[k], sb_s.at[k], sb_r.at[k], (ctx, sibling))
-        copy.start()
-        sib_copies.append(copy)
-        mine[k] = dot(choose_mine, by_token)
     rs_copies = []
-    for k in range(n_cols):
+
+    def send_sum(k):
         sib_copies[k].wait_recv()
         summed = mine[k] + sib_recv[k].astype(F32)
         mine[k] = summed
@@ -340,6 +378,18 @@
             copy.start()
             rs_copies.append(copy)
 
+    for k in range(n_cols):
+        cols = slice(k * col, (k + 1) * col)
+        by_token = dot(hid[...], cond_wv[:, cols]).astype(BF16)
+        sib_send[k] = dot(choose_sib, by_token).astype(BF16)
+        copy = remote(sib_send.at[k], sib_recv.at[k], sb_s.at[k], sb_r.at[k], (ctx, sibling))
+        copy.start()
+        sib_copies.append(copy)
+        mine[k] = dot(choose_mine, by_token)
+        if k:
+            send_sum(k - 1)
+    send_sum(n_cols - 1)
+
     squares = [jnp.zeros((rows_cap, 1), F32) for _ in range(draws)]
     for k in range(n_cols):
         cols = slice(k * col, (k + 1) * col)
@@ -352,17 +402,20 @@
             lifted = base[rows, cols] + cond
             base[rows, cols] = lifted
             squares[d] = squares[d] + jnp.sum(lifted * lifted, axis=1, keepdims=True)
+    gain = row_of(gain_rows)
     for d in range(draws):
         rows = slice(d * rows_cap, (d + 1) * rows_cap)
         scale = lax.rsqrt(squares[d] / width + 1e-06)
-        normed[rows, :] = (base[rows, :] * scale * gain[...]).astype(BF16)
+        normed[rows, :] = (base[rows, :] * scale * gain).astype(BF16)
     loads[4].wait()
 
     def middle_cols(i, total):
         start = pl.multiple_of(i * 256, 256)
         middle = dot(normed[...], mid_wv[:, pl.ds(start, 256)])
         block = (base[:, pl.ds(start, 256)] + middle / (1.0 + jnp.exp(-middle))).astype(BF16)
-        return total + dot(block, noise_out[pl.ds(start, 256), :])
+        return total + lax.dot_general(
+            block, noise_out[:, pl.ds(start, 256)], (((1,), (1,)), ((), ())), preferred_element_type=F32
+        )
 
     result = lax.fori_loop(0, width // 256, middle_cols, jnp.zeros((draws * rows_cap, latent), F32))
     occupied = jnp.sum(own_slots(), axis=1, keepdims=True)
@@ -401,8 +454,10 @@
     col = width // n_cols
     half = width // 2
     freqs = np.exp(-math.log(10000.0) * np.arange(half, dtype=np.float32) / half).astype(np.float32)
+    lanes = 128
+    latent = targets.shape[1]
     vmem = pl.BlockSpec(memory_space=pltpu.VMEM)
-    hbm = pl.BlockSpec(memory_space=pl.ANY)
+    hbm = pl.BlockSpec(memory_space=pltpu.HBM)
     dma = pltpu.SemaphoreType.DMA
     chain = dma((2, pairs - 1, ROW_PARTS))
     fwd = dma((2, pairs, ROW_PARTS))
@@ -412,28 +467,29 @@
         qkv_w,
         out_w,
         cond_w,
-        bias.reshape(1, -1),
+        bias.reshape(-1, lanes),
         in_w,
         mid_w,
-        noise_out,
-        gain.reshape(1, -1),
-        targets,
-        noise,
-        steps,
+        noise_out.T,
+        gain.reshape(-1, lanes),
+        targets.T,
+        noise.T,
+        steps.T,
         masked.reshape(1, -1),
         routes.reshape(1, -1),
-        jnp.asarray(freqs).reshape(1, -1),
+        jnp.asarray(freqs.reshape(-1, lanes)),
     )
-    specs = [hbm if i in (0, 2, 3, 4, 7) else vmem for i in range(len(ops))]
+    small = [pltpu.VMEM(ops[i].shape, ops[i].dtype) for i in (1, 5, 6, 8, 9, 10, 11, 12, 13, 14, 15)]
     return pl.pallas_call(
         functools.partial(kernel, n_ctx, n_grp, cap, rows_cap),
         out_shape=(
             jax.ShapeDtypeStruct(tokens.shape, BF16),
             jax.ShapeDtypeStruct((cap, noise.shape[1]), F32),
         ),
-        in_specs=specs,
+        in_specs=[hbm] * len(ops),
         out_specs=(vmem, vmem),
         scratch_shapes=[
+            *small,
             pltpu.VMEM((n_grp, tok_rows, d_shard), BF16),
             pltpu.VMEM(qkv_w.shape, BF16),
             pltpu.VMEM(out_w.shape, BF16),
@@ -446,6 +502,8 @@
             pltpu.VMEM((tok_rows, 3 * head), F32),
             pltpu.VMEM((draws * rows_cap, width), F32),
             pltpu.VMEM((draws * rows_cap, width), BF16),
+            pltpu.VMEM((rows_cap, draws), F32),
+            pltpu.VMEM((draws * rows_cap, latent), BF16),
             pltpu.VMEM((1, tok_rows), jnp.int32),
             pltpu.VMEM((n_cols, pairs * rows_cap, col), F32),
             pltpu.VMEM((n_cols, pairs * rows_cap, col), BF16),
@@ -453,6 +511,7 @@
             pltpu.VMEM((n_cols, pairs * rows_cap, col), BF16),
             pltpu.VMEM((n_cols, pairs, rows_cap, col), BF16),
             dma((5,)),
+            dma((len(small),)),
             chain,
             chain,
             fwd,
@@ -469,7 +528,7 @@
             dma((n_cols, pairs)),
         ],
         compiler_params=pltpu.CompilerParams(
-            collective_id=0, has_side_effects=True, vmem_limit_bytes=52 * 2**20
+            collective_id=0, has_side_effects=True, vmem_limit_bytes=64 * 2**20 - 2**16
         ),
     )(*ops)
 

time: 83 us -> 75.2 us (0.906)
  local copies, waits for them, and re-layouts: 10.9 us -> 3.11 us
    unnamed x18 -> x2, local copies, waits for them, and re-layouts: 9.46 us -> 3.11 us
    reshape x2 -> x0, local copies, waits for them, and re-layouts: 1.4 us -> none  [the longest x1 0.7 us: shards(): bias.reshape(1, -1)]
where the time goes in v2:
time: 75.2 us; the launch traced here: 75 us
  Pallas kernels  71.2 us (95%)
  local copies, waits for them, and re-layouts  3.11 us (4%)
    pallas_call x1, Pallas kernels, shards(): pl.pallas_call(functools.partial(kernel, n_ctx, n_grp, cap, rows_cap), ou...  71.2 us
    unnamed x2, local copies, waits for them, and re-layouts  3.11 us

profile of v2, /device:TPU:0, one launch (start us, length us, event | category | flops | bytes accessed | tf_op | source)
XLA Modules:
  0.0 75.0 jit_solution(15087270200435447534)
XLA Ops:
  0.6 71.2 %shard_map.167 = (bf16[256,768]{1,0:T(8,128)(2,1)}, f32[48,64]{1,0:T(8,128)}) custom-call(bf16[256,768]{1,0:T(8,128)(2,1)} %tokens.1, s32[1,1024]{1,0:T(1,128)} %bitcast.14, bf16[6144,384]{1,0:T(8,128)(2,1)} %qkv_w.1, bf16[1024,768]{1,0:T(8,128)(2,1)} %out_w.1, bf16[768,1536]{1,0:T(8,128)(2,1)} %cond_w.1, f32[12,128]{1,0:T(8,128)} %bitcast.12, ...), custom_call_target="tpu_custom_call" | custom-call | tf_op jit(solution)/shard_map/pallas_call | solution.py:483
  71.9 1.8 %copy.20 = bf16[256,768]{1,0:T(8,128)(2,1)} copy(bf16[256,768]{1,0:T(8,128)(2,1)} %get-tuple-element.4) | data formatting | bytes 786432
  73.6 1.3 %copy.21 = f32[48,64]{1,0:T(8,128)} copy(f32[48,64]{1,0:T(8,128)} %get-tuple-element.5) | data formatting | bytes 24576
